TPU v7x, 32 devices: a whole 2x2x4 slice. The times are simulated.
32 devices in a mesh: groups: 2 (over y), node: 4 (over z), feat: 4 (over x, core).
Axes of the slice: x: 2, y: 2, z: 4, core: 2. Of those that a mesh axis runs over, the one named last changes fastest.
Arguments:
- features: bfloat16 [32768, 256], P(('groups', 'node'), 'feat'), parts along dimension 0, may hold values from -6 to 6
- weight: bfloat16 [256, 172], P('feat'), may hold values from -24 to 24
- block_cols: int32 [256, 8], P(('groups', 'node')), parts along dimension 0, may hold values from 0 to 127, as said below
- block_live: int32 [256, 8], P(('groups', 'node')), parts along dimension 0, may hold values 0 or 1
- block_tiles: bfloat16 [256, 8, 128, 128], P(('groups', 'node')), parts along dimension 0, may hold values from -0.1875 to 0.1875
- labels: int32 [32768], P(('groups', 'node')), parts along dimension 0, may hold values from 0 to 171
Outputs:
- loss: float32 [2], P('groups'), parts along dimension 0
- weight_grad: float32 [512, 172], P(('groups', 'feat')), parts along dimension 0
- grad_features: bfloat16 [32768, 256], P(('groups', 'node'), 'feat'), parts along dimension 0
There are 2 independent parts, one for each index of `groups`. A program takes and returns all parts, laid end to end along the dimension named above; an argument that names none is the same for every part. Nothing has to cross between parts.
Inputs may be any that keep to these rules, and one draw needn't show every extreme that they name: `block_cols`: the 32 block rows of each index of node name, over their 8 slots, column blocks held at each index of node in exactly 64 slots.
All inputs are finite; a program needn't handle non-finite values. No bound on the sum of `block_live` on one device may be relied on, other than what follows from the above.
Results may differ from a plain program's by a relative error of at most 0.012.
The roundings to bfloat16 on the way count: a program that leaves them out, or rounds other values in their place, can miss the bound.
Values may be sent and summed in bfloat16 or wider, within the bound.
A program may use at most 128 MiB of HBM per device.

v0:
```python
import jax
import jax.numpy as jnp
from jax import lax
from jax.sharding import PartitionSpec as P


def softmax_terms(logits, labels):
    highest = jnp.max(logits, axis=1, keepdims=True)
    totals = jnp.sum(jnp.exp(logits - highest), axis=1, keepdims=True)
    logsum = highest + jnp.log(totals)
    onehot = labels[:, None] == jnp.arange(logits.shape[1], dtype=jnp.int32)[None, :]
    picked = jnp.sum(jnp.where(onehot, logits, 0.0), axis=1, keepdims=True)
    loss_sum = jnp.sum(logsum - picked).reshape(1)
    grad_logits = (jnp.exp(logits - logsum) - onehot.astype(logits.dtype)).astype(jnp.bfloat16)
    return (loss_sum, grad_logits)


def local(features, weight, block_cols, block_live, block_tiles, labels):
    rows_local, feat_width = features.shape
    block_count, slot_count, block_size, _ = block_tiles.shape
    node_parts = lax.axis_size("node")
    live_mask = block_live.astype(jnp.bfloat16)[:, :, None, None]
    whole = lax.all_gather(features, "node", axis=0, tiled=True)
    all_blocks = whole.reshape(whole.shape[0] // block_size, block_size, feat_width)
    panels = jnp.take(all_blocks, block_cols.reshape(-1), axis=0)
    panels = panels.reshape(block_count, slot_count, block_size, feat_width) * live_mask
    summed = jnp.einsum("bskm,bsmf->bkf", block_tiles, panels, preferred_element_type=jnp.float32)
    aggregated = summed.reshape(rows_local, feat_width).astype(jnp.bfloat16)
    node_total = rows_local * node_parts
    partial_logits = jnp.dot(aggregated, weight, preferred_element_type=jnp.float32)
    logits = lax.psum(partial_logits, "feat")
    loss_part, grad_logits = softmax_terms(logits, labels)
    grad_part = jnp.dot(aggregated.T, grad_logits, preferred_element_type=jnp.float32)
    weight_grad, loss_sum = lax.psum((grad_part, loss_part), "node")
    grad_agg = jnp.dot(grad_logits, weight.T, preferred_element_type=jnp.float32).astype(
        jnp.bfloat16
    )
    loss = loss_sum / node_total
    grad_blocks = grad_agg.reshape(block_count, block_size, feat_width)
    contrib = jnp.einsum(
        "bskm,bkf->bsmf", block_tiles, grad_blocks, preferred_element_type=jnp.float32
    )
    contrib = contrib * block_live.astype(jnp.float32)[:, :, None, None]
    flat_contrib = contrib.reshape(block_count * slot_count, block_size, feat_width)
    flat_cols = block_cols.reshape(-1)
    placed = jax.ops.segment_sum(flat_contrib, flat_cols, num_segments=block_count * node_parts)
    placed = placed.reshape(block_count * node_parts * block_size, feat_width)
    grad_sum = lax.psum_scatter(placed, "node", scatter_dimension=0, tiled=True)
    grad_features = grad_sum.astype(jnp.bfloat16)
    return (loss, weight_grad, grad_features)


def solution(mesh):
    placed = (
        P(("groups", "node"), "feat"),
        P("feat", None),
        P(("groups", "node"), None),
        P(("groups", "node"), None),
        P(("groups", "node"), None, None, None),
        P(("groups", "node")),
    )
    return jax.shard_map(
        local,
        mesh=mesh,
        in_specs=placed,
        out_specs=(P("groups"), P(("groups", "feat"), None), P(("groups", "node"), "feat")),
        check_vma=False,
    )
```

profile of v0, /device:TPU:0, one launch (start us, length us, event | category | flops | bytes accessed | tf_op | source)
XLA Modules:
  0.0 284.9 jit_solution(4701934945231811183)
XLA Ops:
  7.2 0.0 copy-start
  7.2 0.0 all-gather.2.cloned.1.call-start
  7.2 0.7 all-gather.2.cloned.1.call-update
  7.9 0.0 all-reduce.3.cloned.1.call-start
  8.0 0.8 copy.23
  8.7 0.7 compare_and_fusion
  9.4 0.1 copy.22
  9.5 0.8 fusion.24
  10.3 0.1 copy.25
  10.4 0.1 reshape.80
  10.5 47.8 %all-gather.2.cloned.1.call-done = bf16[16384,64]{0,1:T(8,128)(2,1)} async-done(((bf16[4096,64]{0,1:T(8,128)(2,1)}), bf16[16384,64]{0,1:T(8,128)(2,1)}) %all-gather.2.cloned.1.call-update) | async-done | bytes 2097168 | tf_op jit(solution)/shard_map/all_gather | solution.py:23
  58.3 2.2 copy_bitcast_fusion.1
  60.4 3.0 %gather_fusion = bf16[256,128,64]{1,2,0:T(8,128)(2,1)} fusion(bf16[128,128,64]{1,2,0:T(8,128)(2,1)S(1)} %copy_bitcast_fusion.1, s32[1024]{0:T(1024)S(1)} %pad_clamp_fusion), kind=kCustom, calls=%fused_computation | custom fusion | bytes 8389632 | tf_op jit(solution)/shard_map/jit(_take)/gather | solution.py:25
  63.5 7.7 %fusion.12 = bf16[32,8,8,128]{3,2,1,0:T(8,128)(2,1)S(1)} fusion(bf16[32,8,128,128]{3,2,1,0:T(8,128)(2,1)} %param.10, bf16[32,8,128,64]{2,3,1,0:T(8,128)(2,1)} %bitcast.43, pred[32,8]{1,0:T(8,128)(4,1)S(1)} %copy.22, bf16[32,8]{1,0:T(8,128)(2,1)S(1)} %copy.25), kind=kOutput, calls=%fused_computation.18 | convolution fusion | flops 541327360 | bytes 13107968 | tf_op jit(solution)/shard_map/bskm,bsmf->bkf/dot_general | solution.py:27
  71.2 0.0 copy-done
  71.2 2.2 fusion.18
  73.4 0.0 copy-start.2
  73.4 0.0 all-reduce.3.cloned.1.call-update
  73.4 0.0 reduce-scatter.2.cloned.1.call-start
  73.4 0.1 reshape.95
  73.5 0.1 copy.29
  73.6 62.8 %all-reduce.3.cloned.1.call-done = f32[4096,172]{0,1:T(8,128)} async-done(((f32[4096,172]{0,1:T(8,128)}), f32[4096,172]{0,1:T(8,128)}) %all-reduce.3.cloned.1.call-update) | async-done | bytes 2818064 | tf_op jit(solution)/shard_map/psum | solution.py:31
  136.4 0.0 copy-start.1
  136.4 2.1 reduce_max.9
  138.6 0.0 copy-done.2
  138.6 0.6 copy-done.1
  139.1 0.8 select_reduce_fusion
  139.9 0.6 subtract_reduce_fusion
  140.5 0.9 fusion.15
  141.4 0.1 copy.38
  141.5 8.4 %broadcast_multiply_fusion = f32[32,64,8,128]{3,1,2,0:T(8,128)} fusion(f32[32,8]{1,0:T(8,128)S(1)} %copy.29, bf16[32,8,128,128]{3,2,1,0:T(8,128)(2,1)} %param.10, bf16[32,128,64,1]{1,0,2,3:T(8,128)(2,1)S(1)} %bitcast.44), kind=kOutput, calls=%fused_computation.4 | convolution fusion | flops 538968064 | bytes 17302528 | tf_op jit(solution)/shard_map/bskm,bkf->bsmf/dot_general | solution.py:40
  149.9 2.5 broadcast_in_dim.27
  152.4 39.3 %scatter_fusion = f32[128,128,64]{1,2,0:T(8,128)} fusion(f32[128,128,64]{1,2,0:T(8,128)} %broadcast_in_dim.27, s32[256]{0:T(256)S(1)} %reshape.95, f32[256,128,64]{1,2,0:T(8,128)} %bitcast.42), kind=kCustom, calls=%fused_computation.1 | custom fusion | flops 2097152 | bytes 25166848 | tf_op jit(solution)/shard_map/scatter-add | solution.py:46
  191.7 4.4 %copy_bitcast_fusion = f32[16384,64]{0,1:T(8,128)} fusion(f32[128,128,64]{1,2,0:T(8,128)} %scatter_fusion), kind=kLoop, calls=%fused_computation.3 | loop fusion | bytes 8388608 | tf_op jit(solution)/shard_map/reshape | solution.py:47
  196.1 0.0 reduce-scatter.2.cloned.1.call-update
  196.1 1.5 fusion.16
  197.6 23.8 %all-reduce = (f32[1]{0:T(128)}, f32[64,172]{1,0:T(8,128)}) all-reduce(f32[1]{0:T(128)} %bitcast.5, f32[64,172]{1,0:T(8,128)} %fusion.16), channel_id=1, replica_groups=mesh['groups'=2,'node'=4,'feat'=4] {'node'}, use_global_device_ids=true, to_apply=%region_5.6 | all-reduce | flops 11009 | bytes 88072 | tf_op jit(solution)/shard_map/psum | solution.py:34
  222.0 53.2 %reduce-scatter.2.cloned.1.call-done = f32[4096,64]{0,1:T(8,128)} async-done(((f32[16384,64]{0,1:T(8,128)}), f32[4096,64]{0,1:T(8,128)}) %reduce-scatter.2.cloned.1.call-update) | async-done | bytes 1048592 | tf_op jit(solution)/shard_map/reduce_scatter | solution.py:48
  275.2 2.1 convert_element_type.35
  (2 shorter events, 0.0 us)
Async XLA Ops:
  7.2 64.0 %copy-start = (bf16[64,172]{1,0:T(8,128)(2,1)S(1)}, bf16[64,172]{1,0:T(8,128)(2,1)}, u32[]{:S(2)}) copy-start(bf16[64,172]{1,0:T(8,128)(2,1)} %param.7) | copy-start | bytes 66052
  7.2 51.1 %all-gather.2.cloned.1.call-start = ((), (), s32[]{:S(2)}) async-start(), calls=%async_computation.1 | async-start | bytes 2621440 | tf_op jit(solution)/shard_map/all_gather | solution.py:23
  7.9 128.5 %all-reduce.3.cloned.1.call-start = ((), (), s32[]{:S(2)}) async-start(), calls=%async_computation.2 | async-start | bytes 5767168 | tf_op jit(solution)/shard_map/psum | solution.py:31
  73.4 65.2 %copy-start.2 = (s32[4096]{0:T(1024)S(1)}, s32[4096]{0:T(1024)}, u32[]{:S(2)}) copy-start(s32[4096]{0:T(1024)} %param.11) | copy-start | bytes 49156
  73.4 201.8 %reduce-scatter.2.cloned.1.call-start = ((), (), s32[]{:S(2)}) async-start(), calls=%async_computation.3 | async-start | bytes 5242880 | tf_op jit(solution)/shard_map/reduce_scatter | solution.py:48
  136.4 2.7 copy-start.1
Sparse Core Ops, SparseCore 0:
  9.6 48.6 all-gather.1
  73.5 62.8 all-reduce.2
  196.2 78.9 reduce-scatter.1
where the time goes:
time: 286 us; the launch traced here: 285 us
  waiting for transfers between devices  164 us (57%)
  other arithmetic  46.3 us (16%)
  blocking collectives  23.8 us (8%)
  matrix products  20.6 us (7%)
  between operations  15.6 us (5%)
  local copies, waits for them, and re-layouts  13.9 us (5%)
    psum x1, waiting for transfers between devices, local(): logits = lax.psum(partial_logits, 'feat')  62.8 us
    reduce_scatter x1, waiting for transfers between devices, local(): grad_sum = lax.psum_scatter(placed, 'node', scatter_dimension=0, tiled=True)  53.2 us
    all_gather x1, waiting for transfers between devices, local(): whole = lax.all_gather(features, 'node', axis=0, tiled=True)  47.8 us
    scatter-add x1, other arithmetic, local(): jax.ops.segment_sum(flat_contrib, flat_cols, num_segments=block_count * n...  39.3 us
    psum x1, blocking collectives, local(): weight_grad, loss_sum = lax.psum((grad_part, loss_part), 'node')  23.8 us
    dot_general x1, matrix products, local(): jnp.einsum('bskm,bkf->bsmf', block_tiles, grad_blocks, preferred_element_...  8.38 us
    dot_general x1, matrix products, local(): jnp.einsum('bskm,bsmf->bkf', block_tiles, panels, preferred_element_type=...  7.7 us
  transfers between devices with their start and end apart: 3, of which 3 were waited for; matrix products, arithmetic and copies ran while one was open for 1% of the time, Pallas kernels for 0%

commit v1 on v0

v1 whole, which is shorter than its diff:
```python
import functools

import jax
import jax.numpy as jnp
from jax import lax
from jax.experimental import pallas as pl
from jax.experimental.pallas import tpu as pltpu
from jax.sharding import PartitionSpec as P

MESH = pl.DeviceIdType.MESH
NT = (((1,), (1,)), ((), ()))
UNROLL = 8


def kernel(dims, *refs):
    n, nf, classes, pad_classes, row_classes, slots = dims
    (x_ref, w_ref, lab_ref, tiles_hbm, order, lcol, rank, live, keep, last, has) = refs[:11]
    loss_ref, wg_ref, gf_ref = refs[11:14]
    rest = list(refs[14:])
    xown = rest.pop(0)
    xr = [rest.pop(0) for _ in range(n - 1)]
    xl = [rest.pop(0) for _ in range(n - 1)]
    (tiles, prod, agg, agr, gsend, gback, wfull, wgs, wgr, wz, wzs, wzr,
     sr, sl, rr, rl, tile_sem, xs_sem, xr_sem, ws_sem, wr_sem, as_sem, ar_sem,
     gs_sem, gr_sem, vs_sem, vr_sem, zs_sem, zr_sem, rs_sem, rv_sem) = rest

    blocks, feat, blk = xown.shape
    share = blocks // nf
    per = order.shape[0] // n
    z = lax.axis_index("node")
    f = lax.axis_index("feat")
    has_right, has_left = z < n - 1, z > 0

    def node_dev(i):
        return {"node": i}

    def feat_dev(i):
        return {"feat": i}

    def send(src, dst, s_sem, r_sem, device):
        return pltpu.make_async_remote_copy(
            src_ref=src, dst_ref=dst, send_sem=s_sem, recv_sem=r_sem,
            device_id=device, device_id_type=MESH)

    tile_copy = pltpu.make_async_copy(tiles_hbm, tiles, tile_sem)
    tile_copy.start()

    barrier = pltpu.get_barrier_semaphore()
    for d in range(1, nf):
        pl.semaphore_signal(barrier, inc=1, device_id=feat_dev(lax.rem(f + d, nf)), device_id_type=MESH)

    @pl.when(has_right)
    def _():
        pl.semaphore_signal(barrier, inc=1, device_id=node_dev(z + 1), device_id_type=MESH)

    @pl.when(has_left)
    def _():
        pl.semaphore_signal(barrier, inc=1, device_id=node_dev(z - 1), device_id_type=MESH)

    for b in range(blocks):
        xown[b] = x_ref[:, b * blk:(b + 1) * blk]
    wfull[f] = w_ref[...]
    pl.semaphore_wait(barrier, nf - 1 + has_right.astype(jnp.int32) + has_left.astype(jnp.int32))

    def x_right(s):
        return send(xown if s == 0 else xr[s - 1], xr[s], xs_sem.at[0, s], xr_sem.at[0, s], node_dev(z + 1))

    def x_left(s):
        return send(xown if s == 0 else xl[s - 1], xl[s], xs_sem.at[1, s], xr_sem.at[1, s], node_dev(z - 1))

    pl.when(has_right)(lambda: x_right(0).start())
    pl.when(has_left)(lambda: x_left(0).start())

    def w_copy(d):
        return send(wfull.at[f], wfull.at[f], ws_sem.at[d - 1], wr_sem.at[d - 1],
                    feat_dev(lax.rem(f + d, nf)))

    for d in range(1, nf):
        w_copy(d).start()

    tile_copy.wait()

    def forward_products(buf, owner):
        base = owner * per

        def body(step, carry):
            for u in range(UNROLL):
                t = base + step * UNROLL + u
                part = lax.dot_general(buf[lcol[t]], tiles[order[t]], NT,
                                       preferred_element_type=jnp.float32)
                prod[t] = part * live[t]
            return carry

        lax.fori_loop(0, per // UNROLL, body, 0)

    forward_products(xown, z)
    for s in range(n - 1):
        @pl.when(z - 1 - s >= 0)
        def _():
            x_right(s).wait_recv()
            if s + 1 < n - 1:
                pl.when(has_right)(lambda: x_right(s + 1).start())

        @pl.when(z + 1 + s < n)
        def _():
            x_left(s).wait_recv()
            if s + 1 < n - 1:
                pl.when(has_left)(lambda: x_left(s + 1).start())

        pl.when(z - 1 - s >= 0)(lambda: forward_products(xr[s], z - 1 - s))
        pl.when(z + 1 + s < n)(lambda: forward_products(xl[s], z + 1 + s))

    def a_copy(d):
        peer = lax.rem(f + d, nf)
        return send(agg.at[pl.ds(peer * share, share)], agr.at[f], as_sem.at[d - 1], ar_sem.at[d - 1],
                    feat_dev(peer))

    def sum_rows(first):
        def body(i, carry):
            row = first + i
            total = prod[rank[row * slots]]
            for s in range(1, slots):
                total = total + prod[rank[row * slots + s]]
            agg[row] = total.astype(jnp.bfloat16)
            return carry

        lax.fori_loop(0, share, body, 0)

    for d in list(range(nf - 1, 0, -1)):
        sum_rows(lax.rem(f + d, nf) * share)
        a_copy(d).start()
    sum_rows(f * share)
    agr[f] = agg[pl.ds(f * share, share)]

    for d in range(1, nf):
        w_copy(d).wait_recv()
    w_all = jnp.concatenate([wfull[i] for i in range(nf)], axis=0)
    w_turned = w_all.astype(jnp.float32).T.astype(jnp.bfloat16)[:row_classes]
    for d in range(1, nf):
        a_copy(d).wait_recv()

    class_row = lax.broadcasted_iota(jnp.int32, (row_classes, 2 * blk), 0)
    loss_row = jnp.zeros((1, 2 * blk), jnp.float32)
    wg = None
    for b in range(0, share, 2):
        part = jnp.concatenate(
            [jnp.concatenate([agr[i, b + c] for i in range(nf)], axis=0) for c in range(2)], axis=1)
        logits = jnp.dot(w_turned, part, preferred_element_type=jnp.float32)
        logits = jnp.where(class_row < classes, logits, -3e38)
        label = jnp.concatenate([lab_ref[pl.ds(f * share + b + c, 1), :] for c in range(2)], axis=1)
        onehot = class_row == label
        highest = jnp.max(logits, axis=0, keepdims=True)
        grown = jnp.exp(logits - highest)
        total = jnp.sum(grown, axis=0, keepdims=True)
        picked = jnp.sum(jnp.where(onehot, logits, 0.0), axis=0, keepdims=True)
        loss_row = loss_row + (highest + jnp.log(total) - picked)
        grad = grown * (1.0 / total) - jnp.where(onehot, 1.0, 0.0)
        grad = grad.astype(jnp.bfloat16)
        grad = jnp.concatenate(
            [grad, jnp.zeros((pad_classes - row_classes, 2 * blk), jnp.bfloat16)], axis=0)
        back = jnp.dot(w_all, grad, preferred_element_type=jnp.float32).astype(jnp.bfloat16)
        for i in range(nf):
            for c in range(2):
                gsend[i, b + c] = back[i * feat:(i + 1) * feat, c * blk:(c + 1) * blk]
        more = lax.dot_general(part, grad, NT, preferred_element_type=jnp.float32)
        wg = more if wg is None else wg + more

    def g_copy(d):
        peer = lax.rem(f + d, nf)
        return send(gsend.at[peer], gback.at[pl.ds(f * share, share)], gs_sem.at[d - 1], gr_sem.at[d - 1],
                    feat_dev(peer))

    def v_copy(d):
        peer = lax.rem(f + d, nf)
        return send(wgs.at[peer], wgr.at[d - 1], vs_sem.at[d - 1], vr_sem.at[d - 1], feat_dev(peer))

    for d in range(nf - 1, 0, -1):
        g_copy(d).start()
    for i in range(nf):
        wgs[i, :feat] = wg[i * feat:(i + 1) * feat]
        wgs[i, feat:] = jnp.broadcast_to(loss_row, (8, 2 * blk))
    for d in range(nf - 1, 0, -1):
        v_copy(d).start()
    gback[pl.ds(f * share, share)] = gsend[f]
    for d in range(1, nf):
        g_copy(d).wait_recv()

    def backward_products(owner):
        base = owner * per

        def body(step, total):
            for u in range(UNROLL):
                i = step * UNROLL + u
                t = base + i
                slot = order[t]
                part = jnp.dot(gback[lax.div(slot, slots)], tiles[slot],
                               preferred_element_type=jnp.float32)
                total = part * live[t] + total * keep[t]
                prod[i] = total
            return total

        lax.fori_loop(0, per // UNROLL, body, jnp.zeros((feat, blk), jnp.float32))

    def right_copy(k):
        return send(sr.at[k], rr.at[k], rs_sem.at[0, k], rv_sem.at[0, k], node_dev(z + 1))

    def left_copy(k):
        return send(sl.at[k], rl.at[k], rs_sem.at[1, k], rv_sem.at[1, k], node_dev(z - 1))

    def fill(out, came, owner):
        def body(j, carry):
            at = owner * blocks + j
            total = prod[last[at]] * has[at]
            if came is not None:
                total = total + came[j].astype(jnp.float32)
            out[j] = total.astype(jnp.bfloat16)
            return carry

        lax.fori_loop(0, blocks, body, 0)

    def z_right():
        return send(wzs.at[0], wzr.at[0], zs_sem.at[0], zr_sem.at[0], node_dev(z + 1))

    def z_left():
        return send(wzs.at[1], wzr.at[1], zs_sem.at[1], zr_sem.at[1], node_dev(z - 1))

    for k in range(n - 1):
        @pl.when(n - 1 - k > z)
        def _():
            owner = n - 1 - k
            backward_products(owner)

            @pl.when(has_left)
            def _():
                right_copy(k).wait_recv()
                fill(sr.at[k], rr.at[k], owner)

            pl.when(jnp.logical_not(has_left))(lambda: fill(sr.at[k], None, owner))
            right_copy(k).start()

        @pl.when(k < z)
        def _():
            backward_products(k)

            @pl.when(has_right)
            def _():
                left_copy(k).wait_recv()
                fill(sl.at[k], rl.at[k], k)

            pl.when(jnp.logical_not(has_right))(lambda: fill(sl.at[k], None, k))
            left_copy(k).start()

        if k == 0:
            own = wgs[f]
            for d in range(1, nf):
                v_copy(d).wait_recv()
                own = own + wgr[d - 1]
            wz[...] = own

            @pl.when(jnp.logical_not(has_left))
            def _():
                wzs[0] = wz[...]
                z_right().start()

            @pl.when(jnp.logical_not(has_right))
            def _():
                wzs[1] = wz[...]
                z_left().start()

        if k == min(1, n - 2):
            @pl.when(has_left)
            def _():
                z_right().wait_recv()

                @pl.when(has_right)
                def _():
                    wzs[0] = wz[...] + wzr[0]
                    z_right().start()

            @pl.when(has_right)
            def _():
                z_left().wait_recv()

                @pl.when(has_left)
                def _():
                    wzs[1] = wz[...] + wzr[1]
                    z_left().start()

    backward_products(z)

    pl.when(has_left)(lambda: right_copy(n - 1 - z).wait_recv())
    pl.when(has_right)(lambda: left_copy(z).wait_recv())
    one = jnp.where(has_left, 1.0, 0.0)
    two = jnp.where(has_right, 1.0, 0.0)

    @pl.when(jnp.logical_not(has_left))
    def _():
        rr[n - 1 - z] = jnp.zeros(rr.shape[1:], rr.dtype)
        wzr[0] = jnp.zeros(wzr.shape[1:], wzr.dtype)

    @pl.when(jnp.logical_not(has_right))
    def _():
        rl[z] = jnp.zeros(rl.shape[1:], rl.dtype)
        wzr[1] = jnp.zeros(wzr.shape[1:], wzr.dtype)

    for j in range(blocks):
        at = z * blocks + j
        total = prod[last[at]] * has[at]
        total = total + rr[n - 1 - z, j].astype(jnp.float32) + rl[z, j].astype(jnp.float32)
        gf_ref[:, j * blk:(j + 1) * blk] = total.astype(jnp.bfloat16)

    full = wz[...] + wzr[0] + wzr[1]
    wg_ref[...] = full[:feat, :classes]
    mean = jnp.sum(full[feat:feat + 1], axis=1, keepdims=True) / (n * blocks * blk)
    loss_ref[...] = jnp.broadcast_to(mean, loss_ref.shape)

    for s in range(n - 1):
        pl.when(jnp.logical_and(has_right, z - s >= 0))(lambda: x_right(s).wait_send())
        pl.when(jnp.logical_and(has_left, z + s < n))(lambda: x_left(s).wait_send())
        pl.when(n - 1 - s > z)(lambda: right_copy(s).wait_send())
        pl.when(s < z)(lambda: left_copy(s).wait_send())
    for d in range(1, nf):
        w_copy(d).wait_send()
        a_copy(d).wait_send()
        g_copy(d).wait_send()
        v_copy(d).wait_send()
    pl.when(has_right)(lambda: z_right().wait_send())
    pl.when(has_left)(lambda: z_left().wait_send())


def slot_lists(block_cols, block_live, n):
    blocks = block_cols.shape[0]
    cols = block_cols.reshape(-1)
    live = block_live.reshape(-1)
    count = cols.shape[0]
    spot = jnp.arange(count, dtype=jnp.int32)
    key = cols * count + spot
    rank = jnp.sum((key[None, :] < key[:, None]).astype(jnp.int32), axis=1)
    match = rank[None, :] == spot[:, None]
    order = jnp.sum(jnp.where(match, spot[None, :], 0), axis=1)
    sorted_cols = jnp.sum(jnp.where(match, cols[None, :], 0), axis=1)
    sorted_live = jnp.sum(jnp.where(match, live[None, :], 0), axis=1).astype(jnp.float32)
    lcol = lax.rem(sorted_cols, blocks)
    keep = jnp.concatenate([jnp.zeros((1,), jnp.bool_), sorted_cols[1:] == sorted_cols[:-1]])
    keep = keep.astype(jnp.float32)
    targets = jnp.arange(blocks * n, dtype=jnp.int32)
    upto = jnp.sum((cols[None, :] <= targets[:, None]).astype(jnp.int32), axis=1)
    has = jnp.any(cols[None, :] == targets[:, None], axis=1)
    last = jnp.where(has, lax.rem(upto - 1, count // n), 0)
    return order, lcol, rank, sorted_live, keep, last, has.astype(jnp.float32)


def local(features, weight, block_cols, block_live, block_tiles, labels):
    n, nf = lax.axis_size("node"), lax.axis_size("feat")
    rows, feat = features.shape
    blocks, slots, blk, _ = block_tiles.shape
    classes = weight.shape[1]
    pad_classes = 256 * pl.cdiv(classes, 256)
    row_classes = 16 * pl.cdiv(classes, 16)
    share = blocks // nf
    lists = slot_lists(block_cols, block_live, n)
    wide = jnp.pad(weight, ((0, 0), (0, pad_classes - classes)))
    bf, f32 = jnp.bfloat16, jnp.float32
    vmem = pl.BlockSpec(memory_space=pltpu.VMEM)
    smem = pl.BlockSpec(memory_space=pltpu.SMEM)
    panel = (blocks, feat, blk)
    dma = pltpu.SemaphoreType.DMA
    scratch = [pltpu.VMEM(panel, bf) for _ in range(2 * n - 1)] + [
        pltpu.VMEM((blocks * slots, blk, blk), bf),
        pltpu.VMEM((blocks * slots, feat, blk), f32),
        pltpu.VMEM(panel, bf),
        pltpu.VMEM((nf, share, feat, blk), bf),
        pltpu.VMEM((nf, share, feat, blk), bf),
        pltpu.VMEM(panel, bf),
        pltpu.VMEM((nf, feat, pad_classes), bf),
        pltpu.VMEM((nf, feat + 8, pad_classes), f32),
        pltpu.VMEM((nf - 1, feat + 8, pad_classes), f32),
        pltpu.VMEM((feat + 8, pad_classes), f32),
        pltpu.VMEM((2, feat + 8, pad_classes), f32),
        pltpu.VMEM((2, feat + 8, pad_classes), f32),
        pltpu.VMEM((n - 1,) + panel, bf),
        pltpu.VMEM((n - 1,) + panel, bf),
        pltpu.VMEM((n,) + panel, bf),
        pltpu.VMEM((n,) + panel, bf),
        dma, dma((2, n - 1)), dma((2, n - 1)),
        dma((nf - 1,)), dma((nf - 1,)), dma((nf - 1,)), dma((nf - 1,)),
        dma((nf - 1,)), dma((nf - 1,)), dma((nf - 1,)), dma((nf - 1,)),
        dma((2,)), dma((2,)), dma((2, n)), dma((2, n)),
    ]
    loss, weight_grad, turned = pl.pallas_call(
        functools.partial(kernel, (n, nf, classes, pad_classes, row_classes, slots)),
        out_shape=(
            jax.ShapeDtypeStruct((8, 128), f32),
            jax.ShapeDtypeStruct((feat, classes), f32),
            jax.ShapeDtypeStruct((feat, rows), bf),
        ),
        in_specs=[vmem, vmem, vmem, pl.BlockSpec(memory_space=pl.ANY)] + [smem] * 7,
        out_specs=(vmem, vmem, vmem),
        scratch_shapes=scratch,
        compiler_params=pltpu.CompilerParams(
            collective_id=0, has_side_effects=True, vmem_limit_bytes=56 * 1024 * 1024),
    )(features.T, wide, labels.reshape(blocks, blk),
      block_tiles.reshape(blocks * slots, blk, blk), *lists)
    return loss[0, :1], weight_grad, turned.T


def solution(mesh):
    placed = (
        P(("groups", "node"), "feat"),
        P("feat", None),
        P(("groups", "node"), None),
        P(("groups", "node"), None),
        P(("groups", "node"), None, None, None),
        P(("groups", "node")),
    )
    return jax.shard_map(
        local,
        mesh=mesh,
        in_specs=placed,
        out_specs=(P("groups"), P(("groups", "feat"), None), P(("groups", "node"), "feat")),
        check_vma=False,
    )
```

time: 286 us -> 142 us (0.50)
  waiting for transfers between devices: 164 us -> 0 us
  Pallas kernels: 0 us -> 129 us
  other arithmetic: 46.3 us -> 4.15 us
  blocking collectives: 23.8 us -> 0 us
  matrix products: 20.6 us -> 0 us
  between operations: 15.6 us -> 0.66 us
  local copies, waits for them, and re-layouts: 13.9 us -> 7.62 us
    pallas_call x0 -> x1, Pallas kernels: none -> 129 us  [local(): pl.pallas_call(functools.partial(kernel, (n, nf, classes, pad_classes, ro...]
    psum x1 -> x0, waiting for transfers between devices: 62.8 us -> none  [local(): logits = lax.psum(partial_logits, 'feat')]
    reduce_scatter x1 -> x0, waiting for transfers between devices: 53.2 us -> none  [local(): grad_sum = lax.psum_scatter(placed, 'node', scatter_dimension=0, tiled=True)]
    all_gather x1 -> x0, waiting for transfers between devices: 47.8 us -> none  [local(): whole = lax.all_gather(features, 'node', axis=0, tiled=True)]
    scatter-add x1 -> x0, other arithmetic: 39.3 us -> none  [local(): jax.ops.segment_sum(flat_contrib, flat_cols, num_segments=block_count * n...]
    psum x1 -> x0, blocking collectives: 23.8 us -> none  [local(): weight_grad, loss_sum = lax.psum((grad_part, loss_part), 'node')]
    dot_general x5 -> x0, matrix products: 20.6 us -> none  [the longest x1 8.38 us: local(): jnp.einsum('bskm,bkf->bsmf', block_tiles, grad_blocks, preferred_element_...]
    reshape x4 -> x1, local copies, waits for them, and re-layouts: 6.73 us -> 0.09 us  [slot_lists(): cols = block_cols.reshape(-1)]
  transfers between devices with their start and end apart: 3 -> 0, of which waited for: 3 -> 0; matrix products, arithmetic and copies ran while one was open for 1% -> 0% of each run, Pallas kernels for 0% -> 0%
where the time goes in v1:
time: 142 us; the launch traced here: 141 us
  Pallas kernels  129 us (91%)
  local copies, waits for them, and re-layouts  7.62 us (5%)
  other arithmetic  4.15 us (3%)
    pallas_call x1, Pallas kernels, local(): pl.pallas_call(functools.partial(kernel, (n, nf, classes, pad_classes, ro...  129 us
    unnamed x6, local copies, waits for them, and re-layouts  4.87 us

profile of v1, /device:TPU:0, one launch (start us, length us, event | category | flops | bytes accessed | tf_op | source)
XLA Modules:
  0.0 141.1 jit_solution(8511470066747105846)
XLA Ops:
  0.6 0.8 copy.11
  1.4 0.1 reshape.38
  1.5 0.1 fusion
  1.6 0.6 convert_element_type.21.refs_10_
  2.2 0.1 convert_reduce_fusion.1
  2.3 0.5 fusion.3.refs_9_
  2.8 0.2 convert_reduce_fusion.refs_6_
  3.0 0.0 copy-start
  3.0 0.8 copy.12
  3.8 0.1 broadcast_in_dim.38
  3.9 0.8 select_reduce_fusion
  4.7 0.6 convert_element_type.18.refs_7_
  5.2 0.1 slice_compare_fusion
  5.3 0.6 compare_select_fusion.2.refs_5_
  5.9 0.6 add_convert_fusion.refs_8_
  6.5 1.4 pad.4.refs_1_
  7.9 0.0 copy-done
  7.9 128.7 %shard_map.85 = (f32[8,128]{1,0:T(8,128)}, f32[64,172]{1,0:T(8,128)}, bf16[64,4096]{1,0:T(8,128)(2,1)}) custom-call(bf16[64,4096]{1,0:T(8,128)(2,1)} %bitcast.6, bf16[64,256]{1,0:T(8,128)(2,1)} %pad.4.refs_1_, s32[32,128]{1,0:T(8,128)} %bitcast.8, bf16[256,128,128]{2,1,0:T(8,128)(2,1)} %bitcast.5, s32[256]{0:T(256)} %get-tuple-element.11.refs_4_, ...), custom_call_target="tpu_custom_call" | custom-call | tf_op jit(solution)/shard_map/pallas_call | solution.py:390
  136.6 1.2 slice.11
  137.8 1.5 %copy.15 = f32[64,172]{1,0:T(8,128)} copy(f32[64,172]{1,0:T(8,128)} %get-tuple-element.16) | data formatting | bytes 88064
  139.2 1.9 %copy.16 = bf16[4096,64]{0,1:T(8,128)(2,1)} copy(bf16[4096,64]{0,1:T(8,128)(2,1)} %bitcast.7) | data formatting | bytes 1048576
  (1 shorter events, 0.0 us)
Async XLA Ops:
  3.0 4.9 %copy-start = (s32[256]{0:T(256)}, s32[256]{0:T(256)S(1)}, u32[]{:S(2)}) copy-start(s32[256]{0:T(256)S(1)} %convert_reduce_fusion.refs_6_) | copy-start | bytes 3076

commit v2 on v1

--- a/solution.py
+++ b/solution.py
@@ -14,19 +14,20 @@
 
 def kernel(dims, *refs):
     n, nf, classes, pad_classes, row_classes, slots = dims
-    (x_ref, w_ref, lab_ref, tiles_hbm, order, lcol, rank, live, keep, last, has) = refs[:11]
-    loss_ref, wg_ref, gf_ref = refs[11:14]
-    rest = list(refs[14:])
+    (x_ref, w_ref, lab_ref, slot_ref, tiles_hbm) = refs[:5]
+    loss_ref, wg_ref, gf_ref = refs[5:8]
+    rest = list(refs[8:])
     xown = rest.pop(0)
     xr = [rest.pop(0) for _ in range(n - 1)]
     xl = [rest.pop(0) for _ in range(n - 1)]
     (tiles, prod, agg, agr, gsend, gback, wfull, wgs, wgr, wz, wzs, wzr,
      sr, sl, rr, rl, tile_sem, xs_sem, xr_sem, ws_sem, wr_sem, as_sem, ar_sem,
-     gs_sem, gr_sem, vs_sem, vr_sem, zs_sem, zr_sem, rs_sem, rv_sem) = rest
+     gs_sem, gr_sem, vs_sem, vr_sem, zs_sem, zr_sem, rs_sem, rv_sem,
+     found, ends, lists, tops, list_sem) = rest
 
     blocks, feat, blk = xown.shape
     share = blocks // nf
-    per = order.shape[0] // n
+    per = blocks * slots // n
     z = lax.axis_index("node")
     f = lax.axis_index("feat")
     has_right, has_left = z < n - 1, z > 0
@@ -59,7 +60,8 @@
 
     for b in range(blocks):
         xown[b] = x_ref[:, b * blk:(b + 1) * blk]
-    wfull[f] = w_ref[...]
+    wfull[f] = jnp.concatenate(
+        [w_ref[...], jnp.zeros((feat, pad_classes - classes), jnp.bfloat16)], axis=1)
     pl.semaphore_wait(barrier, nf - 1 + has_right.astype(jnp.int32) + has_left.astype(jnp.int32))
 
     def x_right(s):
@@ -78,6 +80,14 @@
     for d in range(1, nf):
         w_copy(d).start()
 
+    found[...], ends[...] = slot_lists(slot_ref[...], blocks, n)
+    list_copy = pltpu.make_async_copy(found, lists, list_sem.at[0])
+    top_copy = pltpu.make_async_copy(ends, tops, list_sem.at[1])
+    list_copy.start()
+    top_copy.start()
+    list_copy.wait()
+    top_copy.wait()
+
     tile_copy.wait()
 
     def forward_products(buf, owner):
@@ -86,9 +96,9 @@
         def body(step, carry):
             for u in range(UNROLL):
                 t = base + step * UNROLL + u
-                part = lax.dot_general(buf[lcol[t]], tiles[order[t]], NT,
+                part = lax.dot_general(buf[lists[1, t]], tiles[lists[0, t]], NT,
                                        preferred_element_type=jnp.float32)
-                prod[t] = part * live[t]
+                prod[t] = part * lists[3, t].astype(jnp.float32)
             return carry
 
         lax.fori_loop(0, per // UNROLL, body, 0)
@@ -118,9 +128,9 @@
     def sum_rows(first):
         def body(i, carry):
             row = first + i
-            total = prod[rank[row * slots]]
+            total = prod[lists[2, row * slots]]
             for s in range(1, slots):
-                total = total + prod[rank[row * slots + s]]
+                total = total + prod[lists[2, row * slots + s]]
             agg[row] = total.astype(jnp.bfloat16)
             return carry
 
@@ -192,10 +202,10 @@
             for u in range(UNROLL):
                 i = step * UNROLL + u
                 t = base + i
-                slot = order[t]
+                slot = lists[0, t]
                 part = jnp.dot(gback[lax.div(slot, slots)], tiles[slot],
                                preferred_element_type=jnp.float32)
-                total = part * live[t] + total * keep[t]
+                total = part * lists[3, t].astype(jnp.float32) + total * lists[4, t].astype(jnp.float32)
                 prod[i] = total
             return total
 
@@ -210,7 +220,7 @@
     def fill(out, came, owner):
         def body(j, carry):
             at = owner * blocks + j
-            total = prod[last[at]] * has[at]
+            total = prod[tops[0, at]] * tops[1, at].astype(jnp.float32)
             if came is not None:
                 total = total + came[j].astype(jnp.float32)
             out[j] = total.astype(jnp.bfloat16)
@@ -224,33 +234,36 @@
     def z_left():
         return send(wzs.at[1], wzr.at[1], zs_sem.at[1], zr_sem.at[1], node_dev(z - 1))
 
-    for k in range(n - 1):
-        @pl.when(n - 1 - k > z)
+    for tick in range(n - 1):
+        kr = tick - z
+        kl = tick - (n - 1 - z)
+
+        @pl.when(kr >= 0)
         def _():
-            owner = n - 1 - k
+            owner = n - 1 - kr
             backward_products(owner)
 
             @pl.when(has_left)
             def _():
-                right_copy(k).wait_recv()
-                fill(sr.at[k], rr.at[k], owner)
-
-            pl.when(jnp.logical_not(has_left))(lambda: fill(sr.at[k], None, owner))
-            right_copy(k).start()
-
-        @pl.when(k < z)
+                right_copy(kr).wait_recv()
+                fill(sr.at[kr], rr.at[kr], owner)
+
+            pl.when(jnp.logical_not(has_left))(lambda: fill(sr.at[kr], None, owner))
+            right_copy(kr).start()
+
+        @pl.when(kl >= 0)
         def _():
-            backward_products(k)
+            backward_products(kl)
 
             @pl.when(has_right)
             def _():
-                left_copy(k).wait_recv()
-                fill(sl.at[k], rl.at[k], k)
-
-            pl.when(jnp.logical_not(has_right))(lambda: fill(sl.at[k], None, k))
-            left_copy(k).start()
-
-        if k == 0:
+                left_copy(kl).wait_recv()
+                fill(sl.at[kl], rl.at[kl], kl)
+
+            pl.when(jnp.logical_not(has_right))(lambda: fill(sl.at[kl], None, kl))
+            left_copy(kl).start()
+
+        if tick == 0:
             own = wgs[f]
             for d in range(1, nf):
                 v_copy(d).wait_recv()
@@ -267,31 +280,21 @@
                 wzs[1] = wz[...]
                 z_left().start()
 
-        if k == min(1, n - 2):
-            @pl.when(has_left)
+            @pl.when(jnp.logical_and(has_left, has_right))
             def _():
                 z_right().wait_recv()
-
-                @pl.when(has_right)
-                def _():
-                    wzs[0] = wz[...] + wzr[0]
-                    z_right().start()
-
-            @pl.when(has_right)
-            def _():
+                wzs[0] = wz[...] + wzr[0]
+                z_right().start()
                 z_left().wait_recv()
-
-                @pl.when(has_left)
-                def _():
-                    wzs[1] = wz[...] + wzr[1]
-                    z_left().start()
+                wzs[1] = wz[...] + wzr[1]
+                z_left().start()
 
     backward_products(z)
 
     pl.when(has_left)(lambda: right_copy(n - 1 - z).wait_recv())
     pl.when(has_right)(lambda: left_copy(z).wait_recv())
-    one = jnp.where(has_left, 1.0, 0.0)
-    two = jnp.where(has_right, 1.0, 0.0)
+    pl.when(jnp.logical_not(has_right))(lambda: z_right().wait_recv())
+    pl.when(jnp.logical_not(has_left))(lambda: z_left().wait_recv())
 
     @pl.when(jnp.logical_not(has_left))
     def _():
@@ -305,7 +308,7 @@
 
     for j in range(blocks):
         at = z * blocks + j
-        total = prod[last[at]] * has[at]
+        total = prod[tops[0, at]] * tops[1, at].astype(jnp.float32)
         total = total + rr[n - 1 - z, j].astype(jnp.float32) + rl[z, j].astype(jnp.float32)
         gf_ref[:, j * blk:(j + 1) * blk] = total.astype(jnp.bfloat16)
 
@@ -328,26 +331,35 @@
     pl.when(has_left)(lambda: z_left().wait_send())
 
 
-def slot_lists(block_cols, block_live, n):
-    blocks = block_cols.shape[0]
-    cols = block_cols.reshape(-1)
-    live = block_live.reshape(-1)
-    count = cols.shape[0]
-    spot = jnp.arange(count, dtype=jnp.int32)
-    key = cols * count + spot
-    rank = jnp.sum((key[None, :] < key[:, None]).astype(jnp.int32), axis=1)
-    match = rank[None, :] == spot[:, None]
-    order = jnp.sum(jnp.where(match, spot[None, :], 0), axis=1)
-    sorted_cols = jnp.sum(jnp.where(match, cols[None, :], 0), axis=1)
-    sorted_live = jnp.sum(jnp.where(match, live[None, :], 0), axis=1).astype(jnp.float32)
-    lcol = lax.rem(sorted_cols, blocks)
-    keep = jnp.concatenate([jnp.zeros((1,), jnp.bool_), sorted_cols[1:] == sorted_cols[:-1]])
-    keep = keep.astype(jnp.float32)
-    targets = jnp.arange(blocks * n, dtype=jnp.int32)
-    upto = jnp.sum((cols[None, :] <= targets[:, None]).astype(jnp.int32), axis=1)
-    has = jnp.any(cols[None, :] == targets[:, None], axis=1)
-    last = jnp.where(has, lax.rem(upto - 1, count // n), 0)
-    return order, lcol, rank, sorted_live, keep, last, has.astype(jnp.float32)
+def slot_lists(packed, blocks, n):
+    count = packed.shape[1]
+    down = lax.broadcasted_iota(jnp.int32, (count, count), 0)
+    across = lax.broadcasted_iota(jnp.int32, (count, count), 1)
+
+    def upright(row):
+        return jnp.sum(jnp.where(down == across, row, 0), axis=1, keepdims=True)
+
+    cols, live = lax.shift_right_logical(packed, 1), packed & 1
+    key = cols * count + across[:1]
+    key_up, cols_up, live_up = upright(key), upright(cols), upright(live)
+    rank = jnp.sum((key_up < key).astype(jnp.int32), axis=0, keepdims=True)
+    match = upright(rank) == across
+
+    def in_order(values_up):
+        return jnp.sum(jnp.where(match, values_up, 0), axis=0, keepdims=True)
+
+    order, sorted_cols = in_order(down), in_order(cols_up)
+    sorted_up = upright(sorted_cols)
+    before = jnp.sum(jnp.where(down + 1 == across, sorted_up, 0), axis=0, keepdims=True)
+    keep = jnp.where(across[:1] > 0, (before == sorted_cols).astype(jnp.int32), 0)
+    lcol = sorted_cols % blocks
+    found = jnp.concatenate([order, lcol, rank, in_order(live_up), keep, keep, keep, keep], axis=0)
+    target = lax.broadcasted_iota(jnp.int32, (count, blocks * n), 1)
+    upto = jnp.sum((cols_up <= target).astype(jnp.int32), axis=0, keepdims=True)
+    has = jnp.max((cols_up == target).astype(jnp.int32), axis=0, keepdims=True)
+    last = jnp.where(has > 0, (upto - 1) % (count // n), 0)
+    ends = jnp.concatenate([last, has, has, has, has, has, has, has], axis=0)
+    return found, ends
 
 
 def local(features, weight, block_cols, block_live, block_tiles, labels):
@@ -358,11 +370,11 @@
     pad_classes = 256 * pl.cdiv(classes, 256)
     row_classes = 16 * pl.cdiv(classes, 16)
     share = blocks // nf
-    lists = slot_lists(block_cols, block_live, n)
-    wide = jnp.pad(weight, ((0, 0), (0, pad_classes - classes)))
+    packed = (block_cols * 2 + block_live).reshape(1, blocks * slots)
+    i32 = jnp.int32
+    count = blocks * slots
     bf, f32 = jnp.bfloat16, jnp.float32
     vmem = pl.BlockSpec(memory_space=pltpu.VMEM)
-    smem = pl.BlockSpec(memory_space=pltpu.SMEM)
     panel = (blocks, feat, blk)
     dma = pltpu.SemaphoreType.DMA
     scratch = [pltpu.VMEM(panel, bf) for _ in range(2 * n - 1)] + [
@@ -386,6 +398,8 @@
         dma((nf - 1,)), dma((nf - 1,)), dma((nf - 1,)), dma((nf - 1,)),
         dma((nf - 1,)), dma((nf - 1,)), dma((nf - 1,)), dma((nf - 1,)),
         dma((2,)), dma((2,)), dma((2, n)), dma((2, n)),
+        pltpu.VMEM((8, count), i32), pltpu.VMEM((8, blocks * n), i32),
+        pltpu.SMEM((8, count), i32), pltpu.SMEM((8, blocks * n), i32), dma((2,)),
     ]
     loss, weight_grad, turned = pl.pallas_call(
         functools.partial(kernel, (n, nf, classes, pad_classes, row_classes, slots)),
@@ -394,13 +408,13 @@
             jax.ShapeDtypeStruct((feat, classes), f32),
             jax.ShapeDtypeStruct((feat, rows), bf),
         ),
-        in_specs=[vmem, vmem, vmem, pl.BlockSpec(memory_space=pl.ANY)] + [smem] * 7,
+        in_specs=[vmem, vmem, vmem, vmem, pl.BlockSpec(memory_space=pl.ANY)],
         out_specs=(vmem, vmem, vmem),
         scratch_shapes=scratch,
         compiler_params=pltpu.CompilerParams(
             collective_id=0, has_side_effects=True, vmem_limit_bytes=56 * 1024 * 1024),
-    )(features.T, wide, labels.reshape(blocks, blk),
-      block_tiles.reshape(blocks * slots, blk, blk), *lists)
+    )(features.T, weight, labels.reshape(blocks, blk), packed,
+      block_tiles.reshape(blocks * slots, blk, blk))
     return loss[0, :1], weight_grad, turned.T
 
 

time: 142 us -> 117 us (0.82)
  the two profiles are of different devices: /device:TPU:0 before, /device:TPU:8 now
where the time goes in v2:
time: 117 us
  Pallas kernels  110 us (94%)
  local copies, waits for them, and re-layouts  5.26 us (4%)
    pallas_call x1, Pallas kernels, local(): pl.pallas_call(functools.partial(kernel, (n, nf, classes, pad_classes, ro...  110 us
    unnamed x2, local copies, waits for them, and re-layouts  3.34 us

profile of v2, /device:TPU:8, one launch (start us, length us, event | category | flops | bytes accessed | tf_op | source)
XLA Modules:
  0.0 117.0 jit_solution(14412258065649197941)
XLA Ops:
  0.6 0.7 multiply_add_fusion
  1.3 0.1 copy.10
  1.4 0.7 reshape.16.refs_3_
  2.1 110.4 %shard_map.85 = (f32[8,128]{1,0:T(8,128)}, f32[64,172]{1,0:T(8,128)}, bf16[64,4096]{1,0:T(8,128)(2,1)}) custom-call(bf16[64,4096]{1,0:T(8,128)(2,1)} %bitcast.6, bf16[64,172]{1,0:T(8,128)(2,1)} %refs_1_.1, s32[32,128]{1,0:T(8,128)} %bitcast.8, s32[1,256]{1,0:T(1,128)} %reshape.16.refs_3_, bf16[256,128,128]{2,1,0:T(8,128)(2,1)} %bitcast.5), custom_call_target="tpu_custom_call" | custom-call | tf_op jit(solution)/shard_map/pallas_call | solution.py:404
  112.5 1.2 %slice.3 = f32[1,1]{1,0:T(1,128)} slice(f32[8,128]{1,0:T(8,128)} %get-tuple-element.6), slice={[0:1], [0:1]} | slice | bytes 8 | tf_op jit(solution)/shard_map/slice | solution.py:418
  113.7 1.5 %copy.13 = f32[64,172]{1,0:T(8,128)} copy(f32[64,172]{1,0:T(8,128)} %get-tuple-element.13) | data formatting | bytes 88064
  115.1 1.9 %copy.14 = bf16[4096,64]{0,1:T(8,128)(2,1)} copy(bf16[4096,64]{0,1:T(8,128)(2,1)} %bitcast.7) | data formatting | bytes 1048576

commit v3 on v2

--- a/solution.py
+++ b/solution.py
@@ -9,7 +9,8 @@
 
 MESH = pl.DeviceIdType.MESH
 NT = (((1,), (1,)), ((), ()))
-UNROLL = 8
+UNROLL = 16
+HALVES = 2
 
 
 def kernel(dims, *refs):
@@ -28,6 +29,8 @@
     blocks, feat, blk = xown.shape
     share = blocks // nf
     per = blocks * slots // n
+    unroll = min(UNROLL, per)
+    half = blocks // HALVES
     z = lax.axis_index("node")
     f = lax.axis_index("feat")
     has_right, has_left = z < n - 1, z > 0
@@ -64,14 +67,20 @@
         [w_ref[...], jnp.zeros((feat, pad_classes - classes), jnp.bfloat16)], axis=1)
     pl.semaphore_wait(barrier, nf - 1 + has_right.astype(jnp.int32) + has_left.astype(jnp.int32))
 
-    def x_right(s):
-        return send(xown if s == 0 else xr[s - 1], xr[s], xs_sem.at[0, s], xr_sem.at[0, s], node_dev(z + 1))
-
-    def x_left(s):
-        return send(xown if s == 0 else xl[s - 1], xl[s], xs_sem.at[1, s], xr_sem.at[1, s], node_dev(z - 1))
-
-    pl.when(has_right)(lambda: x_right(0).start())
-    pl.when(has_left)(lambda: x_left(0).start())
+    def part(ref, h):
+        return ref.at[pl.ds(h * half, half)]
+
+    def x_right(s, h):
+        return send(part(xown if s == 0 else xr[s - 1], h), part(xr[s], h),
+                    xs_sem.at[0, s, h], xr_sem.at[0, s, h], node_dev(z + 1))
+
+    def x_left(s, h):
+        return send(part(xown if s == 0 else xl[s - 1], h), part(xl[s], h),
+                    xs_sem.at[1, s, h], xr_sem.at[1, s, h], node_dev(z - 1))
+
+    for h in range(HALVES):
+        pl.when(has_right)(lambda: x_right(0, h).start())
+        pl.when(has_left)(lambda: x_left(0, h).start())
 
     def w_copy(d):
         return send(wfull.at[f], wfull.at[f], ws_sem.at[d - 1], wr_sem.at[d - 1],
@@ -94,28 +103,29 @@
         base = owner * per
 
         def body(step, carry):
-            for u in range(UNROLL):
-                t = base + step * UNROLL + u
-                part = lax.dot_general(buf[lists[1, t]], tiles[lists[0, t]], NT,
+            for u in range(unroll):
+                t = base + step * unroll + u
+                product = lax.dot_general(buf[lists[1, t]], tiles[lists[0, t]], NT,
                                        preferred_element_type=jnp.float32)
-                prod[t] = part * lists[3, t].astype(jnp.float32)
+                prod[t] = product * lists[3, t].astype(jnp.float32)
             return carry
 
-        lax.fori_loop(0, per // UNROLL, body, 0)
+        lax.fori_loop(0, per // unroll, body, 0)
 
     forward_products(xown, z)
     for s in range(n - 1):
-        @pl.when(z - 1 - s >= 0)
-        def _():
-            x_right(s).wait_recv()
-            if s + 1 < n - 1:
-                pl.when(has_right)(lambda: x_right(s + 1).start())
-
-        @pl.when(z + 1 + s < n)
-        def _():
-            x_left(s).wait_recv()
-            if s + 1 < n - 1:
-                pl.when(has_left)(lambda: x_left(s + 1).start())
+        for h in range(HALVES):
+            @pl.when(z - 1 - s >= 0)
+            def _():
+                x_right(s, h).wait_recv()
+                if s + 1 < n - 1:
+                    pl.when(has_right)(lambda: x_right(s + 1, h).start())
+
+            @pl.when(z + 1 + s < n)
+            def _():
+                x_left(s, h).wait_recv()
+                if s + 1 < n - 1:
+                    pl.when(has_left)(lambda: x_left(s + 1, h).start())
 
         pl.when(z - 1 - s >= 0)(lambda: forward_products(xr[s], z - 1 - s))
         pl.when(z + 1 + s < n)(lambda: forward_products(xl[s], z + 1 + s))
@@ -136,7 +146,8 @@
 
         lax.fori_loop(0, share, body, 0)
 
-    for d in list(range(nf - 1, 0, -1)):
+    far_first = sorted(range(1, nf), key=lambda d: abs(d - nf // 2))
+    for d in far_first:
         sum_rows(lax.rem(f + d, nf) * share)
         a_copy(d).start()
     sum_rows(f * share)
@@ -153,9 +164,9 @@
     loss_row = jnp.zeros((1, 2 * blk), jnp.float32)
     wg = None
     for b in range(0, share, 2):
-        part = jnp.concatenate(
+        whole = jnp.concatenate(
             [jnp.concatenate([agr[i, b + c] for i in range(nf)], axis=0) for c in range(2)], axis=1)
-        logits = jnp.dot(w_turned, part, preferred_element_type=jnp.float32)
+        logits = jnp.dot(w_turned, whole, preferred_element_type=jnp.float32)
         logits = jnp.where(class_row < classes, logits, -3e38)
         label = jnp.concatenate([lab_ref[pl.ds(f * share + b + c, 1), :] for c in range(2)], axis=1)
         onehot = class_row == label
@@ -172,7 +183,7 @@
         for i in range(nf):
             for c in range(2):
                 gsend[i, b + c] = back[i * feat:(i + 1) * feat, c * blk:(c + 1) * blk]
-        more = lax.dot_general(part, grad, NT, preferred_element_type=jnp.float32)
+        more = lax.dot_general(whole, grad, NT, preferred_element_type=jnp.float32)
         wg = more if wg is None else wg + more
 
     def g_copy(d):
@@ -184,12 +195,12 @@
         peer = lax.rem(f + d, nf)
         return send(wgs.at[peer], wgr.at[d - 1], vs_sem.at[d - 1], vr_sem.at[d - 1], feat_dev(peer))
 
-    for d in range(nf - 1, 0, -1):
+    for d in far_first:
         g_copy(d).start()
     for i in range(nf):
         wgs[i, :feat] = wg[i * feat:(i + 1) * feat]
         wgs[i, feat:] = jnp.broadcast_to(loss_row, (8, 2 * blk))
-    for d in range(nf - 1, 0, -1):
+    for d in far_first:
         v_copy(d).start()
     gback[pl.ds(f * share, share)] = gsend[f]
     for d in range(1, nf):
@@ -199,25 +210,25 @@
         base = owner * per
 
         def body(step, total):
-            for u in range(UNROLL):
-                i = step * UNROLL + u
+            for u in range(unroll):
+                i = step * unroll + u
                 t = base + i
                 slot = lists[0, t]
-                part = jnp.dot(gback[lax.div(slot, slots)], tiles[slot],
+                product = jnp.dot(gback[lax.div(slot, slots)], tiles[slot],
                                preferred_element_type=jnp.float32)
-                total = part * lists[3, t].astype(jnp.float32) + total * lists[4, t].astype(jnp.float32)
+                total = product * lists[3, t].astype(jnp.float32) + total * lists[4, t].astype(jnp.float32)
                 prod[i] = total
             return total
 
-        lax.fori_loop(0, per // UNROLL, body, jnp.zeros((feat, blk), jnp.float32))
-
-    def right_copy(k):
-        return send(sr.at[k], rr.at[k], rs_sem.at[0, k], rv_sem.at[0, k], node_dev(z + 1))
-
-    def left_copy(k):
-        return send(sl.at[k], rl.at[k], rs_sem.at[1, k], rv_sem.at[1, k], node_dev(z - 1))
-
-    def fill(out, came, owner):
+        lax.fori_loop(0, per // unroll, body, jnp.zeros((feat, blk), jnp.float32))
+
+    def right_copy(k, h):
+        return send(part(sr.at[k], h), part(rr.at[k], h), rs_sem.at[0, k, h], rv_sem.at[0, k, h], node_dev(z + 1))
+
+    def left_copy(k, h):
+        return send(part(sl.at[k], h), part(rl.at[k], h), rs_sem.at[1, k, h], rv_sem.at[1, k, h], node_dev(z - 1))
+
+    def fill(out, came, owner, h):
         def body(j, carry):
             at = owner * blocks + j
             total = prod[tops[0, at]] * tops[1, at].astype(jnp.float32)
@@ -226,7 +237,17 @@
             out[j] = total.astype(jnp.bfloat16)
             return carry
 
-        lax.fori_loop(0, blocks, body, 0)
+        lax.fori_loop(h * half, (h + 1) * half, body, 0)
+
+    def pass_on(copy, k, out, came, owner, inside):
+        for h in range(HALVES):
+            @pl.when(inside)
+            def _():
+                copy(k, h).wait_recv()
+                fill(out.at[k], came.at[k], owner, h)
+
+            pl.when(jnp.logical_not(inside))(lambda: fill(out.at[k], None, owner, h))
+            copy(k, h).start()
 
     def z_right():
         return send(wzs.at[0], wzr.at[0], zs_sem.at[0], zr_sem.at[0], node_dev(z + 1))
@@ -240,28 +261,13 @@
 
         @pl.when(kr >= 0)
         def _():
-            owner = n - 1 - kr
-            backward_products(owner)
-
-            @pl.when(has_left)
-            def _():
-                right_copy(kr).wait_recv()
-                fill(sr.at[kr], rr.at[kr], owner)
-
-            pl.when(jnp.logical_not(has_left))(lambda: fill(sr.at[kr], None, owner))
-            right_copy(kr).start()
+            backward_products(n - 1 - kr)
+            pass_on(right_copy, kr, sr, rr, n - 1 - kr, has_left)
 
         @pl.when(kl >= 0)
         def _():
             backward_products(kl)
-
-            @pl.when(has_right)
-            def _():
-                left_copy(kl).wait_recv()
-                fill(sl.at[kl], rl.at[kl], kl)
-
-            pl.when(jnp.logical_not(has_right))(lambda: fill(sl.at[kl], None, kl))
-            left_copy(kl).start()
+            pass_on(left_copy, kl, sl, rl, kl, has_right)
 
         if tick == 0:
             own = wgs[f]
@@ -280,19 +286,24 @@
                 wzs[1] = wz[...]
                 z_left().start()
 
-            @pl.when(jnp.logical_and(has_left, has_right))
+        if tick > 0:
+            @pl.when(jnp.logical_and(z == tick, has_right))
             def _():
                 z_right().wait_recv()
                 wzs[0] = wz[...] + wzr[0]
                 z_right().start()
+
+            @pl.when(jnp.logical_and(n - 1 - z == tick, has_left))
+            def _():
                 z_left().wait_recv()
                 wzs[1] = wz[...] + wzr[1]
                 z_left().start()
 
     backward_products(z)
 
-    pl.when(has_left)(lambda: right_copy(n - 1 - z).wait_recv())
-    pl.when(has_right)(lambda: left_copy(z).wait_recv())
+    for h in range(HALVES):
+        pl.when(has_left)(lambda: right_copy(n - 1 - z, h).wait_recv())
+        pl.when(has_right)(lambda: left_copy(z, h).wait_recv())
     pl.when(jnp.logical_not(has_right))(lambda: z_right().wait_recv())
     pl.when(jnp.logical_not(has_left))(lambda: z_left().wait_recv())
 
@@ -318,10 +329,11 @@
     loss_ref[...] = jnp.broadcast_to(mean, loss_ref.shape)
 
     for s in range(n - 1):
-        pl.when(jnp.logical_and(has_right, z - s >= 0))(lambda: x_right(s).wait_send())
-        pl.when(jnp.logical_and(has_left, z + s < n))(lambda: x_left(s).wait_send())
-        pl.when(n - 1 - s > z)(lambda: right_copy(s).wait_send())
-        pl.when(s < z)(lambda: left_copy(s).wait_send())
+        for h in range(HALVES):
+            pl.when(jnp.logical_and(has_right, z - s >= 0))(lambda: x_right(s, h).wait_send())
+            pl.when(jnp.logical_and(has_left, z + s < n))(lambda: x_left(s, h).wait_send())
+            pl.when(n - 1 - s > z)(lambda: right_copy(s, h).wait_send())
+            pl.when(s < z)(lambda: left_copy(s, h).wait_send())
     for d in range(1, nf):
         w_copy(d).wait_send()
         a_copy(d).wait_send()
@@ -394,10 +406,10 @@
         pltpu.VMEM((n - 1,) + panel, bf),
         pltpu.VMEM((n,) + panel, bf),
         pltpu.VMEM((n,) + panel, bf),
-        dma, dma((2, n - 1)), dma((2, n - 1)),
+        dma, dma((2, n - 1, HALVES)), dma((2, n - 1, HALVES)),
         dma((nf - 1,)), dma((nf - 1,)), dma((nf - 1,)), dma((nf - 1,)),
         dma((nf - 1,)), dma((nf - 1,)), dma((nf - 1,)), dma((nf - 1,)),
-        dma((2,)), dma((2,)), dma((2, n)), dma((2, n)),
+        dma((2,)), dma((2,)), dma((2, n, HALVES)), dma((2, n, HALVES)),
         pltpu.VMEM((8, count), i32), pltpu.VMEM((8, blocks * n), i32),
         pltpu.SMEM((8, count), i32), pltpu.SMEM((8, blocks * n), i32), dma((2,)),
     ]

time: 117 us -> 109 us (0.932)
  the two profiles are of different devices: /device:TPU:8 before, /device:TPU:0 now
where the time goes in v3:
time: 109 us; the launch traced here: 108 us
  Pallas kernels  102 us (94%)
  local copies, waits for them, and re-layouts  5.26 us (5%)
    pallas_call x1, Pallas kernels, local(): pl.pallas_call(functools.partial(kernel, (n, nf, classes, pad_classes, ro...  102 us
    unnamed x2, local copies, waits for them, and re-layouts  3.34 us

profile of v3, /device:TPU:0, one launch (start us, length us, event | category | flops | bytes accessed | tf_op | source)
XLA Modules:
  0.0 108.5 jit_solution(12933240572282764894)
XLA Ops:
  0.6 0.7 multiply_add_fusion
  1.3 0.1 copy.10
  1.4 0.7 reshape.16.refs_3_
  2.1 101.8 %shard_map.85 = (f32[8,128]{1,0:T(8,128)}, f32[64,172]{1,0:T(8,128)}, bf16[64,4096]{1,0:T(8,128)(2,1)}) custom-call(bf16[64,4096]{1,0:T(8,128)(2,1)} %bitcast.6, bf16[64,172]{1,0:T(8,128)(2,1)} %refs_1_.1, s32[32,128]{1,0:T(8,128)} %bitcast.8, s32[1,256]{1,0:T(1,128)} %reshape.16.refs_3_, bf16[256,128,128]{2,1,0:T(8,128)(2,1)} %bitcast.5), custom_call_target="tpu_custom_call" | custom-call | tf_op jit(solution)/shard_map/pallas_call | solution.py:416
  103.9 1.2 %slice.3 = f32[1,1]{1,0:T(1,128)} slice(f32[8,128]{1,0:T(8,128)} %get-tuple-element.6), slice={[0:1], [0:1]} | slice | bytes 8 | tf_op jit(solution)/shard_map/slice | solution.py:430
  105.1 1.5 %copy.13 = f32[64,172]{1,0:T(8,128)} copy(f32[64,172]{1,0:T(8,128)} %get-tuple-element.13) | data formatting | bytes 88064
  106.6 1.9 %copy.14 = bf16[4096,64]{0,1:T(8,128)(2,1)} copy(bf16[4096,64]{0,1:T(8,128)(2,1)} %bitcast.7) | data formatting | bytes 1048576

commit v4 on v3

--- a/solution.py
+++ b/solution.py
@@ -15,9 +15,9 @@
 
 def kernel(dims, *refs):
     n, nf, classes, pad_classes, row_classes, slots = dims
-    (x_ref, w_ref, lab_ref, slot_ref, tiles_hbm) = refs[:5]
-    loss_ref, wg_ref, gf_ref = refs[5:8]
-    rest = list(refs[8:])
+    (x_ref, w_ref, lab_ref, col_ref, live_ref, tiles_hbm) = refs[:6]
+    loss_ref, wg_ref, gf_ref = refs[6:9]
+    rest = list(refs[9:])
     xown = rest.pop(0)
     xr = [rest.pop(0) for _ in range(n - 1)]
     xl = [rest.pop(0) for _ in range(n - 1)]
@@ -89,7 +89,7 @@
     for d in range(1, nf):
         w_copy(d).start()
 
-    found[...], ends[...] = slot_lists(slot_ref[...], blocks, n)
+    found[...], ends[...] = slot_lists(col_ref[...] * 2 + live_ref[...], n)
     list_copy = pltpu.make_async_copy(found, lists, list_sem.at[0])
     top_copy = pltpu.make_async_copy(ends, tops, list_sem.at[1])
     list_copy.start()
@@ -138,9 +138,9 @@
     def sum_rows(first):
         def body(i, carry):
             row = first + i
-            total = prod[lists[2, row * slots]]
+            total = prod[lists[2, row]]
             for s in range(1, slots):
-                total = total + prod[lists[2, row * slots + s]]
+                total = total + prod[lists[2, s * blocks + row]]
             agg[row] = total.astype(jnp.bfloat16)
             return carry
 
@@ -343,8 +343,10 @@
     pl.when(has_left)(lambda: z_left().wait_send())
 
 
-def slot_lists(packed, blocks, n):
-    count = packed.shape[1]
+def slot_lists(table, n):
+    slots, blocks = table.shape
+    count = slots * blocks
+    packed = jnp.concatenate([table[s:s + 1] for s in range(slots)], axis=1)
     down = lax.broadcasted_iota(jnp.int32, (count, count), 0)
     across = lax.broadcasted_iota(jnp.int32, (count, count), 1)
 
@@ -360,7 +362,7 @@
     def in_order(values_up):
         return jnp.sum(jnp.where(match, values_up, 0), axis=0, keepdims=True)
 
-    order, sorted_cols = in_order(down), in_order(cols_up)
+    order, sorted_cols = in_order(down % blocks * slots + down // blocks), in_order(cols_up)
     sorted_up = upright(sorted_cols)
     before = jnp.sum(jnp.where(down + 1 == across, sorted_up, 0), axis=0, keepdims=True)
     keep = jnp.where(across[:1] > 0, (before == sorted_cols).astype(jnp.int32), 0)
@@ -374,6 +376,12 @@
     return found, ends
 
 
+def hand_over(loss_in, wg_in, gf_in, loss_ref, wg_ref, gf_ref):
+    loss_ref[0] = loss_in[0, 0]
+    wg_ref[...] = wg_in[...]
+    gf_ref[...] = gf_in[...]
+
+
 def local(features, weight, block_cols, block_live, block_tiles, labels):
     n, nf = lax.axis_size("node"), lax.axis_size("feat")
     rows, feat = features.shape
@@ -382,7 +390,6 @@
     pad_classes = 256 * pl.cdiv(classes, 256)
     row_classes = 16 * pl.cdiv(classes, 16)
     share = blocks // nf
-    packed = (block_cols * 2 + block_live).reshape(1, blocks * slots)
     i32 = jnp.int32
     count = blocks * slots
     bf, f32 = jnp.bfloat16, jnp.float32
@@ -420,14 +427,25 @@
             jax.ShapeDtypeStruct((feat, classes), f32),
             jax.ShapeDtypeStruct((feat, rows), bf),
         ),
-        in_specs=[vmem, vmem, vmem, vmem, pl.BlockSpec(memory_space=pl.ANY)],
+        in_specs=[vmem, vmem, vmem, vmem, vmem, pl.BlockSpec(memory_space=pl.ANY)],
         out_specs=(vmem, vmem, vmem),
         scratch_shapes=scratch,
         compiler_params=pltpu.CompilerParams(
             collective_id=0, has_side_effects=True, vmem_limit_bytes=56 * 1024 * 1024),
-    )(features.T, weight, labels.reshape(blocks, blk), packed,
+    )(features.T, weight, labels.reshape(blocks, blk), block_cols.T, block_live.T,
       block_tiles.reshape(blocks * slots, blk, blk))
-    return loss[0, :1], weight_grad, turned.T
+    smem = pl.BlockSpec(memory_space=pltpu.SMEM)
+    loss, weight_grad, turned = pl.pallas_call(
+        hand_over,
+        out_shape=(
+            jax.ShapeDtypeStruct((1,), f32),
+            jax.ShapeDtypeStruct((feat, classes), f32),
+            jax.ShapeDtypeStruct((feat, rows), bf),
+        ),
+        in_specs=[smem, vmem, vmem],
+        out_specs=(smem, vmem, vmem),
+    )(loss, weight_grad, turned)
+    return loss, weight_grad, turned.T
 
 
 def solution(mesh):

time: 109 us -> 105 us (0.963)
  local copies, waits for them, and re-layouts: 5.26 us -> 0 us
  Pallas kernels: 102 us -> 104 us
    unnamed x2 -> x0, local copies, waits for them, and re-layouts: 3.34 us -> none
    pallas_call x0 -> x1, Pallas kernels: none -> 1.93 us  [local(): pl.pallas_call(hand_over, out_shape=(jax.ShapeDtypeStruct((1,), f32), jax...]
    slice x1 -> x0, local copies, waits for them, and re-layouts: 1.19 us -> none  [local(): return (loss[0, :1], weight_grad, turned.T)]
where the time goes in v4:
time: 105 us; the launch traced here: 104 us
  Pallas kernels  104 us (99%)
    pallas_call x1, Pallas kernels, local(): pl.pallas_call(functools.partial(kernel, (n, nf, classes, pad_classes, ro...  102 us

profile of v4, /device:TPU:0, one launch (start us, length us, event | category | flops | bytes accessed | tf_op | source)
XLA Modules:
  0.0 104.4 jit_solution(2010192121866747984)
XLA Ops:
  0.6 101.9 %shard_map.85 = (f32[8,128]{1,0:T(8,128)}, f32[64,172]{1,0:T(8,128)}, bf16[64,4096]{1,0:T(8,128)(2,1)}) custom-call(bf16[64,4096]{1,0:T(8,128)(2,1)} %bitcast.7, bf16[64,172]{1,0:T(8,128)(2,1)} %refs_1_.1, s32[32,128]{1,0:T(8,128)} %bitcast.8, s32[8,32]{1,0:T(8,128)} %bitcast.9, s32[8,32]{1,0:T(8,128)} %bitcast.10, bf16[256,128,128]{2,1,0:T(8,128)(2,1)} %bitcast.6), custom_call_target="tpu_custom_call" | custom-call | tf_op jit(solution)/shard_map/pallas_call | solution.py:423
  102.5 1.9 %shard_map.86 = (f32[1]{0:T(128)}, f32[64,172]{1,0:T(8,128)}, bf16[64,4096]{1,0:T(8,128)(2,1)}) custom-call(f32[8,128]{1,0:T(8,128)} %get-tuple-element.9.loss_in, f32[64,172]{1,0:T(8,128)} %get-tuple-element.10.wg_in, bf16[64,4096]{1,0:T(8,128)(2,1)} %get-tuple-element.11.gf_in), custom_call_target="tpu_custom_call" | custom-call | tf_op jit(solution)/shard_map/pallas_call | solution.py:438

commit v5 on v4

--- a/solution.py
+++ b/solution.py
@@ -9,7 +9,7 @@
 
 MESH = pl.DeviceIdType.MESH
 NT = (((1,), (1,)), ((), ()))
-UNROLL = 16
+UNROLL = 32
 HALVES = 2
 
 
@@ -144,7 +144,7 @@
             agg[row] = total.astype(jnp.bfloat16)
             return carry
 
-        lax.fori_loop(0, share, body, 0)
+        lax.fori_loop(0, share, body, 0, unroll=2)
 
     far_first = sorted(range(1, nf), key=lambda d: abs(d - nf // 2))
     for d in far_first:
@@ -237,7 +237,7 @@
             out[j] = total.astype(jnp.bfloat16)
             return carry
 
-        lax.fori_loop(h * half, (h + 1) * half, body, 0)
+        lax.fori_loop(h * half, (h + 1) * half, body, 0, unroll=4)
 
     def pass_on(copy, k, out, came, owner, inside):
         for h in range(HALVES):

time: 105 us -> 103 us (0.981)
    pallas_call x1, Pallas kernels: 102 us -> 101 us  [local(): pl.pallas_call(functools.partial(kernel, (n, nf, classes, pad_classes, ro...]
where the time goes in v5:
time: 103 us
  Pallas kernels  103 us (100%)
    pallas_call x1, Pallas kernels, local(): pl.pallas_call(functools.partial(kernel, (n, nf, classes, pad_classes, ro...  101 us

profile of v5, /device:TPU:0, one launch (start us, length us, event | category | flops | bytes accessed | tf_op | source)
XLA Modules:
  0.0 103.3 jit_solution(3139951271282847014)
XLA Ops:
  0.6 100.7 %shard_map.85 = (f32[8,128]{1,0:T(8,128)}, f32[64,172]{1,0:T(8,128)}, bf16[64,4096]{1,0:T(8,128)(2,1)}) custom-call(bf16[64,4096]{1,0:T(8,128)(2,1)} %bitcast.7, bf16[64,172]{1,0:T(8,128)(2,1)} %refs_1_.1, s32[32,128]{1,0:T(8,128)} %bitcast.8, s32[8,32]{1,0:T(8,128)} %bitcast.9, s32[8,32]{1,0:T(8,128)} %bitcast.10, bf16[256,128,128]{2,1,0:T(8,128)(2,1)} %bitcast.6), custom_call_target="tpu_custom_call" | custom-call | tf_op jit(solution)/shard_map/pallas_call | solution.py:423
  101.3 1.9 %shard_map.86 = (f32[1]{0:T(128)}, f32[64,172]{1,0:T(8,128)}, bf16[64,4096]{1,0:T(8,128)(2,1)}) custom-call(f32[8,128]{1,0:T(8,128)} %get-tuple-element.9.loss_in, f32[64,172]{1,0:T(8,128)} %get-tuple-element.10.wg_in, bf16[64,4096]{1,0:T(8,128)(2,1)} %get-tuple-element.11.gf_in), custom_call_target="tpu_custom_call" | custom-call | tf_op jit(solution)/shard_map/pallas_call | solution.py:438
